TPU v7x, 32 devices: a whole 2x2x4 slice. The times are simulated.
32 devices in a mesh: gx: 4 (over y, x), gy: 8 (over z, core).
Axes of the slice: x: 2, y: 2, z: 4, core: 2. Of those that a mesh axis runs over, the one named last changes fastest.
Arguments:
- a_blocks: bfloat16 [2048, 8, 9216], P(('gx', 'gy')), may hold values from -2 to 2
- a_cols: int32 [2048, 8], P(('gx', 'gy')), may hold values from 0 to 63
- q_blocks: bfloat16 [2048, 9216], P(('gx', 'gy')), may hold values from -0.625 to 0.625
- part_of: int32 [2048, 8], P(('gx', 'gy')), may hold values from 0 to 63
- part_dest: int32 [2048, 1], P(('gx', 'gy')), may hold values from 0 to 7; in each aligned block of 64 rows (0 to 63, 64 to 127, ...) at most 16 rows name the same one
- part_pos: int32 [2048], P(('gx', 'gy')), may hold values from 0 to 15
- g_level: float32 [3, 9216], replicated, may hold values from -0.625 to 0.625
Outputs:
- coarse_first: float32 [64, 8, 9216], P(('gx', 'gy'))
- coarsest: float32 [64, 8, 9216], P(('gx', 'gy'))
Inputs may be any that keep to these rules, and one draw needn't show every extreme that they name: `part_dest`: among the partial blocks of one device at most 16 name the same gy index, and some device's blocks name one index exactly 16 times.
All inputs are finite; a program needn't handle non-finite values.
Results may differ from a plain program's by a relative error of at most 0.0029.
Values sent between devices are 32-bit elements; how exact they have to be, the bound alone decides.
A program may use at most 128 MiB of HBM per device.

v0:
```python
import jax
import jax.numpy as jnp
from jax import lax
from jax.sharding import PartitionSpec as P

B = 96
KA = 8
RC = 2
SC = 8
NP = 64


def partner_2(shard, axis, stride):
    return lax.ppermute(shard, axis, [(i, i ^ 1 << stride) for i in range(lax.axis_size(axis))])


def project(blocks, gmat):
    shaped = blocks.reshape(blocks.shape[0], B, B)
    right = jnp.einsum("mab,bj->maj", shaped, gmat, precision=lax.Precision.HIGHEST)
    result = jnp.einsum("ai,maj->mij", gmat, right, precision=lax.Precision.HIGHEST)
    return result.reshape(blocks.shape[0], B * B)


def select_sum(labels, count, values):
    table = (jnp.arange(count, dtype=jnp.int32)[:, None] == labels[None, :]).astype(jnp.float32)
    return jnp.dot(table, values, precision=lax.Precision.HIGHEST)


def local(a_blocks, a_cols, q_blocks, part_of, part_dest, part_pos, g_level):
    rows = a_blocks.shape[0]
    width = B * B
    cells = RC * SC
    n_inner = lax.axis_size("gy")
    qmats = q_blocks.reshape(rows, B, B)
    picked = q_blocks[a_cols.reshape(-1)].reshape(rows, KA, B, B)
    aq_rows = jnp.einsum(
        "rkij,rkjl->rkil",
        a_blocks.reshape(rows, KA, B, B),
        picked,
        preferred_element_type=jnp.float32,
    ).astype(jnp.bfloat16)
    terms = jnp.einsum("rji,rkjl->rkil", qmats, aq_rows, preferred_element_type=jnp.float32)
    partial_value = select_sum(part_of.reshape(-1), NP, terms.reshape(rows * KA, width))
    target = part_dest[:, 0]
    dense = select_sum(target * cells + part_pos, n_inner * cells, partial_value)
    coarse = lax.psum_scatter(dense, "gy", scatter_dimension=0, tiled=True)
    gmats = g_level.reshape(3, B, B)
    merged = coarse
    for level_bit in range(2):
        partner = partner_2(merged, "gy", level_bit)
        merged = project(merged + partner, gmats[level_bit])
    merged = lax.psum(merged, "gx")
    merged = project(merged, gmats[2])
    return (coarse.reshape(RC, SC, width), merged.reshape(RC, SC, width))


def solution(mesh):
    placed = (
        P(("gx", "gy"), None, None),
        P(("gx", "gy"), None),
        P(("gx", "gy"), None),
        P(("gx", "gy"), None),
        P(("gx", "gy"), None),
        P(("gx", "gy")),
        P(),
    )
    return jax.shard_map(
        local,
        mesh=mesh,
        in_specs=placed,
        out_specs=(P(("gx", "gy"), None, None), P(("gx", "gy"), None, None)),
        check_vma=False,
    )
```

profile of v0, /device:TPU:16, one launch (start us, length us, event | category | flops | bytes accessed | tf_op | source)
XLA Modules:
  0.0 284.5 jit_solution(11541793749306693470)
XLA Ops:
  7.2 0.0 copy-start
  7.2 0.0 reduce-scatter.2.cloned.1.call-start
  7.2 0.9 copy.10
  8.1 0.1 reshape.76
  8.2 2.6 reshape.96
  10.8 0.0 copy-done
  10.8 8.7 %gather_fusion = bf16[512,9216]{1,0:T(8,128)(2,1)} fusion(bf16[64,9216]{1,0:T(8,128)(2,1)S(1)} %copy-done, s32[1024]{0:T(1024)S(1)} %pad_clamp_fusion), kind=kCustom, calls=%fused_computation | custom fusion | bytes 18876416 | tf_op jit(solution)/shard_map/gather | solution.py:35
  19.5 18.7 %reshape.77 = bf16[64,8,96,96]{3,2,1,0:T(8,128)(2,1)} reshape(bf16[512,9216]{1,0:T(8,128)(2,1)} %gather_fusion) | data formatting | bytes 18874368 | tf_op jit(solution)/shard_map/reshape | solution.py:35
  38.2 18.6 %reshape.78 = bf16[64,8,96,96]{3,2,1,0:T(8,128)(2,1)} reshape(bf16[64,8,9216]{2,1,0:T(8,128)(2,1)} %param.7) | data formatting | bytes 18874368 | tf_op jit(solution)/shard_map/reshape | solution.py:38
  56.8 22.4 %fusion.5 = f32[64,8,96,96]{2,3,1,0:T(8,128)} fusion(bf16[64,8,96,96]{3,2,1,0:T(8,128)(2,1)} %reshape.77, bf16[64,8,96,96]{3,2,1,0:T(8,128)(2,1)} %reshape.78, bf16[64,96,96,1]{2,1,0,3:T(8,128)(2,1)S(1)} %reshape.96), kind=kOutput, calls=%fused_computation.5 | convolution fusion | flops 1816657920 | bytes 38928384 | tf_op jit(solution)/shard_map/rji,rkjl->rkil/dot_general | solution.py:42
  79.3 24.7 %copy.11 = f32[64,8,96,96]{3,2,1,0:T(8,128)} copy(f32[64,8,96,96]{2,3,1,0:T(8,128)} %fusion.5) | data formatting | bytes 37748736 | tf_op jit(solution)/shard_map/rji,rkjl->rkil/transpose | solution.py:42
  103.9 24.4 %reshape.80 = f32[512,9216]{1,0:T(8,128)} reshape(f32[64,8,96,96]{3,2,1,0:T(8,128)} %copy.11) | data formatting | bytes 37748736 | tf_op jit(solution)/shard_map/reshape | solution.py:43
  128.3 0.0 copy-done.2
  128.3 0.1 copy.9
  128.4 0.1 eq.32
  128.5 0.0 copy-start.1
  128.5 11.5 %fusion.9 = f32[64,9216]{1,0:T(8,128)S(1)} fusion(f32[512,9216]{1,0:T(8,128)} %reshape.80, s32[512]{0:T(512)S(1)} %eq.32), kind=kOutput, calls=%fused_computation.11 | convolution fusion | flops 3623911424 | bytes 21235712 | tf_op jit(solution)/shard_map/dot_general | solution.py:26
  140.0 0.0 copy-done.3
  140.1 0.0 copy-done.4
  140.1 4.1 %fusion.11 = f32[128,9216]{1,0:T(8,128)} fusion(f32[64,9216]{1,0:T(8,128)S(1)} %fusion.9, s32[64]{0:T(128)S(1)} %bitcast_add_fusion), kind=kOutput, calls=%fused_computation.14 | convolution fusion | flops 905977856 | bytes 7078144 | tf_op jit(solution)/shard_map/dot_general | solution.py:26
  144.2 0.0 reduce-scatter.2.cloned.1.call-update
  144.2 0.0 all-reduce.2.cloned.1.call-start
  144.3 53.6 %reduce-scatter.2.cloned.1.call-done = f32[16,9216]{1,0:T(8,128)} async-done(((f32[128,9216]{1,0:T(8,128)}), f32[16,9216]{1,0:T(8,128)}) %reduce-scatter.2.cloned.1.call-update) | async-done | bytes 589840 | tf_op jit(solution)/shard_map/reduce_scatter | solution.py:46
  197.9 0.8 collective-permute-start
  198.6 0.0 copy-done.1
  198.6 0.3 slice_reduce_fusion
  198.9 0.1 reshape.97
  199.0 1.5 collective-permute-done
  200.5 1.1 add.29
  201.6 0.3 reshape.82
  201.9 1.8 fusion.13
  203.7 0.8 convolution_bitcast_fusion.2
  204.5 0.3 copy.12
  204.8 0.4 reshape.83
  205.2 1.1 collective-permute-start.1
  206.3 0.1 reshape.98
  206.4 14.4 %collective-permute-done.1 = f32[16,9216]{1,0:T(8,128)S(1)} collective-permute-done((f32[16,9216]{1,0:T(8,128)S(1)}, f32[16,9216]{1,0:T(8,128)S(1)}, u32[]{:S(2)}, u32[]{:S(2)}) %collective-permute-start.1) | collective-permute-done | bytes 589856 | tf_op jit(solution)/shard_map/ppermute | solution.py:14
  220.8 0.1 add.30
  220.9 0.3 reshape.84
  221.2 0.8 fusion.14
  222.0 2.3 convolution_bitcast_fusion.1
  224.3 0.0 all-reduce.2.cloned.1.call-update
  224.3 0.1 reshape.99
  224.4 49.1 %all-reduce.2.cloned.1.call-done = f32[16,96,96]{1,2,0:T(8,128)} async-done(((f32[16,96,96]{1,2,0:T(8,128)}), f32[16,96,96]{1,2,0:T(8,128)}) %all-reduce.2.cloned.1.call-update) | async-done | bytes 589840 | tf_op jit(solution)/shard_map/psum | solution.py:52
  273.5 2.0 fusion.15
  275.4 0.8 convolution_bitcast_fusion
  276.2 0.3 copy.13
  276.5 1.2 reshape_reshape.3
  (6 shorter events, 0.0 us)
Async XLA Ops:
  7.2 3.6 %copy-start = (bf16[64,9216]{1,0:T(8,128)(2,1)S(1)}, bf16[64,9216]{1,0:T(8,128)(2,1)}, u32[]{:S(2)}) copy-start(bf16[64,9216]{1,0:T(8,128)(2,1)} %param.9) | copy-start | bytes 3538948
  7.2 190.7 %reduce-scatter.2.cloned.1.call-start = ((), (), s32[]{:S(2)}) async-start(), calls=%async_computation.1 | async-start | bytes 5308416 | tf_op jit(solution)/shard_map/reduce_scatter | solution.py:46
  103.9 24.4 %copy-start.2 = (s32[64,8]{0,1:T(8,128)S(1)}, s32[64,8]{0,1:T(8,128)}, u32[]{:S(2)}) copy-start(s32[64,8]{0,1:T(8,128)} %param.10) | copy-start | bytes 6148
  128.3 11.7 %copy-start.3 = (s32[64]{0:T(128)S(1)}, s32[64]{0:T(128)}, u32[]{:S(2)}) copy-start(s32[64]{0:T(128)} %param.12) | copy-start | bytes 772
  128.3 11.7 %copy-start.4 = (s32[64,1]{0,1:T(1,128)S(1)}, s32[64,1]{0,1:T(1,128)}, u32[]{:S(2)}) copy-start(s32[64,1]{0,1:T(1,128)} %param.11) | copy-start | bytes 772
  128.5 70.1 %copy-start.1 = (f32[3,9216]{1,0:T(4,128)S(1)}, f32[3,9216]{1,0:T(4,128)}, u32[]{:S(2)}) copy-start(f32[3,9216]{1,0:T(4,128)} %param.13) | copy-start | bytes 331780
  144.2 129.3 %all-reduce.2.cloned.1.call-start = ((), (), s32[]{:S(2)}) async-start(), calls=%async_computation.2 | async-start | bytes 1572864 | tf_op jit(solution)/shard_map/psum | solution.py:52
  197.9 2.6 collective-permute-start
  205.2 15.7 %collective-permute-start.1 = (f32[16,9216]{1,0:T(8,128)S(1)}, f32[16,9216]{1,0:T(8,128)S(1)}, u32[]{:S(2)}, u32[]{:S(2)}) collective-permute-start(f32[16,9216]{1,0:T(8,128)S(1)} %reshape.83), channel_id=1, source_target_pairs={{0,2},{1,3},{2,0},{3,1},{4,6},{5,7},{6,4},{7,5},{8,10},{9,11},{10,... | collective-permute-start | bytes 1769480 | tf_op jit(solution)/shard_map/ppermute | solution.py:14
Sparse Core Ops, SparseCore 0:
  144.4 53.4 reduce-scatter.1
  224.4 48.9 all-reduce.1
where the time goes:
time: 288 us; the launch traced here: 285 us
  waiting for transfers between devices  119 us (41%)
  local copies, waits for them, and re-layouts  102 us (35%)
  matrix products  46.5 us (16%)
  between operations  14.2 us (5%)
    reduce_scatter x1, waiting for transfers between devices, local(): coarse = lax.psum_scatter(dense, 'gy', scatter_dimension=0, tiled=True)  53.6 us
    psum x1, waiting for transfers between devices, local(): merged = lax.psum(merged, 'gx')  49.1 us
    transpose x1, local copies, waits for them, and re-layouts, local(): jnp.einsum('rji,rkjl->rkil', qmats, aq_rows, preferred_element_type=jnp.f...  24.7 us
    reshape x1, local copies, waits for them, and re-layouts, local(): terms.reshape(rows * KA, width)  24.4 us
    dot_general x1, matrix products, local(): jnp.einsum('rji,rkjl->rkil', qmats, aq_rows, preferred_element_type=jnp.f...  22.4 us
    reshape x2, local copies, waits for them, and re-layouts, local(): picked = q_blocks[a_cols.reshape(-1)].reshape(rows, KA, B, B)  18.8 us
    reshape x1, local copies, waits for them, and re-layouts, local(): a_blocks.reshape(rows, KA, B, B)  18.6 us
    ppermute x2, waiting for transfers between devices, partner_2(): lax.ppermute(shard, axis, [(i, i ^ 1 << stride) for i in range(lax.axis_s...  15.9 us
  transfers between devices with their start and end apart: 4, of which 4 were waited for; matrix products, arithmetic and copies ran while one was open for 0% of the time, Pallas kernels for 0%

commit v1 on v0

v1 whole, which is shorter than its diff:
```python
import functools

import jax
import jax.numpy as jnp
from jax import lax
from jax.experimental import pallas as pl
from jax.experimental.pallas import tpu as pltpu
from jax.sharding import PartitionSpec as P

B = 96
L = 128
G = 24
RC = 2
SC = 8
ROWS = 8
F32 = jnp.float32
BF16 = jnp.bfloat16


def lanes():
    return lax.broadcasted_iota(jnp.int32, (G, L), 1)


def split_rows(t):
    lane = lanes()
    return [
        t[0],
        pltpu.roll(jnp.where(lane >= 96, t[0], t[1]), 32, 1),
        pltpu.roll(jnp.where(lane >= 64, t[1], t[2]), 64, 1),
        pltpu.roll(t[2], 96, 1),
    ]


def join_rows(c):
    lane = lanes()
    one = pltpu.roll(c[1], 96, 1)
    two = pltpu.roll(c[2], 64, 1)
    three = pltpu.roll(c[3], 32, 1)
    return [
        jnp.where(lane < 96, c[0], one),
        jnp.where(lane < 64, one, two),
        jnp.where(lane < 32, two, three),
    ]


def tiles(ref, at, pitch):
    return [ref[pl.ds(m * pitch + at, G, stride=3 * pitch), :] for m in range(3)]


def products_kernel(
    a_ref, q_ref, g_ref, cols_ref, part_ref, dest_ref, pos_ref, dense_ref, h_ref, a_flat, q_flat, g_flat, nat, q_nat, q_tr, acc
):
    step = pl.program_id(0)
    fine = q_ref.shape[0]
    slots = a_ref.shape[1]
    n_part = acc.shape[0]
    width = a_ref.shape[2] // L

    @pl.when(step == 0)
    def _():
        for u in range(width):
            q_flat[u * fine : (u + 1) * fine, :] = q_ref[:, u * L : (u + 1) * L].astype(F32)
            g_flat[u * 8 : u * 8 + 3, :] = g_ref[:, u * L : (u + 1) * L]
        keep = lax.broadcasted_iota(jnp.int32, (B, L), 1) < B
        q_nat[:, B:, :] = jnp.zeros((fine, L - B, L), BF16)

        def one_q(i, _):
            rows = split_rows(tiles(q_flat, i, fine))
            for r in range(4):
                nat[pl.ds(r, G, stride=4), :] = rows[r]
            q_nat[i, :B, :] = jnp.where(keep, nat[...], 0.0).astype(BF16)
            permuted = jnp.concatenate(rows, axis=0)
            q_tr[i] = jnp.transpose(permuted)[:B].astype(BF16)
            return 0

        lax.fori_loop(0, fine, one_q, 0)

        mats = []
        for l in range(3):
            rows = split_rows(tiles(g_flat, l, 8))
            for r in range(4):
                nat[pl.ds(r, G, stride=4), :] = rows[r]
            mats.append(nat[...][:, :B])
        h = jnp.dot(mats[0], mats[1], precision=lax.Precision.HIGHEST, preferred_element_type=F32)
        h_ref[...] = jnp.dot(h, mats[2], precision=lax.Precision.HIGHEST, preferred_element_type=F32)

        def clear(p, _):
            acc[p] = jnp.zeros((B, L), F32)
            return 0

        lax.fori_loop(0, n_part, clear, 0)

        def clear_dense(p, _):
            dense_ref[pl.ds(p * 128, 128), :] = jnp.zeros((128, L), F32)
            return 0

        lax.fori_loop(0, dense_ref.shape[0] // 128, clear_dense, 0)

    def one_row(rr, slot):
        i = step * ROWS + rr
        flat = a_flat.at[slot]
        for u in range(width):
            flat[u * slots : (u + 1) * slots, :] = a_ref[rr, :, u * L : (u + 1) * L].astype(F32)
        made = []
        for k in range(slots):
            block = jnp.concatenate(split_rows(tiles(flat, k, slots)), axis=0).astype(BF16)
            made.append(jnp.dot(block, q_nat[cols_ref[i, k]], preferred_element_type=F32).astype(BF16))
        term = jnp.dot(q_tr[i], jnp.concatenate(made, axis=1), preferred_element_type=F32)
        for k in range(slots):
            p = part_ref[i, k]
            acc[p] += term[:, k * L : (k + 1) * L]

    def pair(j, _):
        one_row(2 * j, 0)
        one_row(2 * j + 1, 1)
        return 0

    lax.fori_loop(0, ROWS // 2, pair, 0)

    @pl.when(step == pl.num_programs(0) - 1)
    def _():
        cell_rows = width * SC

        def one_part(p, _):
            place = pos_ref[p]
            base = (dest_ref[p, 0] * RC + place // SC) * cell_rows + lax.rem(place, SC)
            flat = join_rows([acc[p, pl.ds(r, G, stride=4), :] for r in range(4)])
            for m in range(3):
                where = pl.ds(base + m * SC, G, stride=3 * SC)
                dense_ref[where, :] = dense_ref[where, :] + flat[m]
            return 0

        lax.fori_loop(0, n_part, one_part, 0)


def products(a_blocks, a_cols, q_blocks, part_of, part_dest, part_pos, g_level, n_inner):
    fine, slots, flat = a_blocks.shape
    n_part = part_pos.shape[0]
    width = flat // L
    smem = pl.BlockSpec(memory_space=pltpu.SMEM)
    vmem = pl.BlockSpec(memory_space=pltpu.VMEM)
    return pl.pallas_call(
        products_kernel,
        grid=(fine // ROWS,),
        out_shape=(
            jax.ShapeDtypeStruct((n_inner * RC * SC * width, L), F32),
            jax.ShapeDtypeStruct((B, B), F32),
        ),
        in_specs=[
            pl.BlockSpec((ROWS, slots, flat), lambda s: (s, 0, 0)),
            vmem,
            vmem,
            smem,
            smem,
            smem,
            smem,
        ],
        out_specs=(vmem, vmem),
        scratch_shapes=[
            pltpu.VMEM((2, width * slots, L), F32),
            pltpu.VMEM((width * fine, L), F32),
            pltpu.VMEM((width * 8, L), F32),
            pltpu.VMEM((B, L), F32),
            pltpu.VMEM((fine, L, L), BF16),
            pltpu.VMEM((fine, B, B), BF16),
            pltpu.VMEM((n_part, B, L), F32),
        ],
        compiler_params=pltpu.CompilerParams(dimension_semantics=("arbitrary",), vmem_limit_bytes=56 * 2**20),
        cost_estimate=pl.CostEstimate(flops=4 * fine * slots * B**3, bytes_accessed=a_blocks.size * 2, transcendentals=0),
    )(a_blocks, q_blocks, g_level, a_cols, part_of, part_dest, part_pos)


def partner_2(shard, axis, stride):
    return lax.ppermute(shard, axis, [(i, i ^ 1 << stride) for i in range(lax.axis_size(axis))])


def local(a_blocks, a_cols, q_blocks, part_of, part_dest, part_pos, g_level):
    flat = a_blocks.shape[2]
    width = flat // L
    n_inner = lax.axis_size("gy")
    dense, h = products(a_blocks, a_cols, q_blocks, part_of, part_dest, part_pos, g_level, n_inner)
    coarse = lax.psum_scatter(dense, "gy", scatter_dimension=0, tiled=True)
    first = coarse.reshape(RC, width, SC, L).transpose(0, 2, 1, 3).reshape(RC, SC, flat)
    total = lax.psum(coarse, "gx")
    for bit in range(2):
        total = total + partner_2(total, "gy", bit)
    total = total.reshape(RC, width, SC, L).transpose(0, 2, 1, 3).reshape(RC * SC, B, B)
    right = jnp.einsum("mab,bj->maj", total, h, precision=lax.Precision.HIGHEST)
    last = jnp.einsum("ai,maj->mij", h, right, precision=lax.Precision.HIGHEST)
    return first, last.reshape(RC, SC, flat)


def solution(mesh):
    placed = (
        P(("gx", "gy"), None, None),
        P(("gx", "gy"), None),
        P(("gx", "gy"), None),
        P(("gx", "gy"), None),
        P(("gx", "gy"), None),
        P(("gx", "gy")),
        P(),
    )
    return jax.shard_map(
        local,
        mesh=mesh,
        in_specs=placed,
        out_specs=(P(("gx", "gy"), None, None), P(("gx", "gy"), None, None)),
        check_vma=False,
    )
```

time: 288 us -> 192 us (0.67)
  local copies, waits for them, and re-layouts: 102 us -> 5.93 us
  Pallas kernels: 0 us -> 44.7 us
  matrix products: 46.5 us -> 2.61 us
    reshape x8 -> x3, local copies, waits for them, and re-layouts: 65.4 us -> 1.55 us  [the longest x1 1.22 us: local(): return (first, last.reshape(RC, SC, flat))]
    pallas_call x0 -> x1, Pallas kernels: none -> 44.7 us  [products(): pl.pallas_call(products_kernel, grid=(fine // ROWS,), out_shape=(jax.Shap...]
    dot_general x9 -> x2, matrix products: 46.5 us -> 2.61 us  [the longest x1 1.84 us: local(): right = jnp.einsum('mab,bj->maj', total, h, precision=lax.Precision.HIGHEST)]
    transpose x3 -> x1, local copies, waits for them, and re-layouts: 25.2 us -> 0.26 us  [local(): last = jnp.einsum('ai,maj->mij', h, right, precision=lax.Precision.HIGHEST)]
    gather x1 -> x0, local copies, waits for them, and re-layouts: 8.67 us -> none  [local(): picked = q_blocks[a_cols.reshape(-1)].reshape(rows, KA, B, B)]
    unnamed x12 -> x5, local copies, waits for them, and re-layouts: 0.96 us -> 4.12 us
where the time goes in v1:
time: 192 us; the launch traced here: 190 us
  waiting for transfers between devices  120 us (62%)
  Pallas kernels  44.7 us (23%)
  between operations  14.1 us (7%)
  local copies, waits for them, and re-layouts  5.93 us (3%)
  matrix products  2.61 us (1%)
    reduce_scatter x1, waiting for transfers between devices, local(): coarse = lax.psum_scatter(dense, 'gy', scatter_dimension=0, tiled=True)  53.6 us
    psum x1, waiting for transfers between devices, local(): total = lax.psum(coarse, 'gx')  50.6 us
    pallas_call x1, Pallas kernels, products(): pl.pallas_call(products_kernel, grid=(fine // ROWS,), out_shape=(jax.Shap...  44.7 us
    ppermute x2, waiting for transfers between devices, partner_2(): lax.ppermute(shard, axis, [(i, i ^ 1 << stride) for i in range(lax.axis_s...  16.1 us
    unnamed x5, local copies, waits for them, and re-layouts  4.12 us
  transfers between devices with their start and end apart: 4, of which 4 were waited for; matrix products, arithmetic and copies ran while one was open for 0% of the time, Pallas kernels for 0%

profile of v1, /device:TPU:16, one launch (start us, length us, event | category | flops | bytes accessed | tf_op | source)
XLA Modules:
  0.0 190.5 jit_solution(14152656950533157039)
XLA Ops:
  7.2 0.0 reduce-scatter.2.cloned.1.call-start
  7.2 1.4 copy.12.cols_ref
  8.6 1.4 copy.13.part_ref
  10.0 1.4 copy.14.dest_ref
  11.3 44.7 %shard_map.86 = (f32[9216,128]{1,0:T(8,128)}, f32[96,96]{1,0:T(8,128)}) custom-call(bf16[64,8,9216]{2,1,0:T(8,128)(2,1)} %a_ref.1, bf16[64,9216]{1,0:T(8,128)(2,1)} %q_ref.1, f32[3,9216]{1,0:T(4,128)} %g_ref.1, s32[64,8]{1,0:T(8,128)} %copy.12.cols_ref, s32[64,8]{1,0:T(8,128)} %copy.13.part_ref, s32[64,1]{1,0:T(8,128)} %copy.14.dest_ref, s32[64]{0:T(128)} %pos_ref.1), custom_call_target="tpu_custom_call" | custom-call | flops 1811939328 | bytes 9437184 | tf_op jit(solution)/shard_map/pallas_call | solution.py:142
  56.1 0.0 copy-start
  56.1 0.0 reduce-scatter.2.cloned.1.call-update
  56.1 0.0 all-reduce.2.cloned.1.call-start
  56.1 53.6 %reduce-scatter.2.cloned.1.call-done = f32[1152,128]{1,0:T(8,128)} async-done(((f32[9216,128]{1,0:T(8,128)}), f32[1152,128]{1,0:T(8,128)}) %reduce-scatter.2.cloned.1.call-update) | async-done | bytes 589840 | tf_op jit(solution)/shard_map/reduce_scatter | solution.py:182
  109.7 0.0 all-reduce.2.cloned.1.call-update
  109.7 50.6 %all-reduce.2.cloned.1.call-done = f32[1152,128]{1,0:T(8,128)} async-done(((f32[1152,128]{1,0:T(8,128)}), f32[1152,128]{1,0:T(8,128)}) %all-reduce.2.cloned.1.call-update) | async-done | bytes 589840 | tf_op jit(solution)/shard_map/psum | solution.py:184
  160.3 0.0 collective-permute-start
  160.3 2.2 %collective-permute-done = f32[1152,128]{1,0:T(8,128)S(1)} collective-permute-done((f32[1152,128]{1,0:T(8,128)}, f32[1152,128]{1,0:T(8,128)S(1)}, u32[]{:S(2)}, u32[]{:S(2)}) %collective-permute-start) | collective-permute-done | bytes 589856 | tf_op jit(solution)/shard_map/ppermute | solution.py:174
  162.5 1.1 add.10
  163.6 1.6 collective-permute-start.1
  165.2 13.9 %collective-permute-done.1 = f32[1152,128]{1,0:T(8,128)S(1)} collective-permute-done((f32[1152,128]{1,0:T(8,128)S(1)}, f32[1152,128]{1,0:T(8,128)S(1)}, u32[]{:S(2)}, u32[]{:S(2)}) %collective-permute-start.1) | collective-permute-done | bytes 589856 | tf_op jit(solution)/shard_map/ppermute | solution.py:174
  179.1 0.1 add.11
  179.1 0.1 copy.18
  179.3 0.2 reshape.22
  179.5 0.0 copy-done
  179.5 1.8 fusion.1
  181.4 0.8 convolution_bitcast_fusion
  182.1 0.3 copy.16
  182.4 1.2 reshape.23
Async XLA Ops:
  7.2 102.5 %reduce-scatter.2.cloned.1.call-start = ((), (), s32[]{:S(2)}) async-start(), calls=%async_computation.1 | async-start | bytes 5308416 | tf_op jit(solution)/shard_map/reduce_scatter | solution.py:182
  56.1 123.4 %copy-start = (f32[96,96]{1,0:T(8,128)S(1)}, f32[96,96]{1,0:T(8,128)}, u32[]{:S(2)}) copy-start(f32[96,96]{1,0:T(8,128)} %get-tuple-element.5) | copy-start | bytes 110596
  56.1 104.2 %all-reduce.2.cloned.1.call-start = ((), (), s32[]{:S(2)}) async-start(), calls=%async_computation.2 | async-start | bytes 1179648 | tf_op jit(solution)/shard_map/psum | solution.py:184
  160.3 2.2 %collective-permute-start = (f32[1152,128]{1,0:T(8,128)}, f32[1152,128]{1,0:T(8,128)S(1)}, u32[]{:S(2)}, u32[]{:S(2)}) collective-permute-start(f32[1152,128]{1,0:T(8,128)} %all-reduce.2.cloned.1.call-done), channel_id=1, source_target_pairs={{0,1},{1,0},{2,3},{3,2},{4,5},{5,4},{6,7},{7,6},{8,9},{9,8},{10,11... | collective-permute-start | bytes 1769480 | tf_op jit(solution)/shard_map/ppermute | solution.py:174
  163.6 15.4 %collective-permute-start.1 = (f32[1152,128]{1,0:T(8,128)S(1)}, f32[1152,128]{1,0:T(8,128)S(1)}, u32[]{:S(2)}, u32[]{:S(2)}) collective-permute-start(f32[1152,128]{1,0:T(8,128)S(1)} %add.10), channel_id=1, source_target_pairs={{0,2},{1,3},{2,0},{3,1},{4,6},{5,7},{6,4},{7,5},{8,10},{9,11},{10,... | collective-permute-start | bytes 1769480 | tf_op jit(solution)/shard_map/ppermute | solution.py:174
Sparse Core Ops, SparseCore 0:
  56.2 53.4 reduce-scatter.1
  113.3 46.9 all-reduce.1

commit v2 on v1

--- a/solution.py
+++ b/solution.py
@@ -48,7 +48,7 @@
 
 
 def products_kernel(
-    a_ref, q_ref, g_ref, cols_ref, part_ref, dest_ref, pos_ref, dense_ref, h_ref, a_flat, q_flat, g_flat, nat, q_nat, q_tr, acc
+    a_ref, q_ref, g_ref, cols_ref, part_ref, dest_ref, pos_ref, dense_ref, h_ref, ht_ref, a_flat, q_flat, g_flat, nat, q_nat, q_tr, acc
 ):
     step = pl.program_id(0)
     fine = q_ref.shape[0]
@@ -82,7 +82,11 @@
                 nat[pl.ds(r, G, stride=4), :] = rows[r]
             mats.append(nat[...][:, :B])
         h = jnp.dot(mats[0], mats[1], precision=lax.Precision.HIGHEST, preferred_element_type=F32)
-        h_ref[...] = jnp.dot(h, mats[2], precision=lax.Precision.HIGHEST, preferred_element_type=F32)
+        h = jnp.dot(h, mats[2], precision=lax.Precision.HIGHEST, preferred_element_type=F32)
+        h_ref[...] = jnp.zeros((L, L), F32)
+        h_ref[:B, :B] = h
+        nat[:, :B] = h
+        ht_ref[...] = jnp.transpose(jnp.concatenate([nat[pl.ds(r, G, stride=4), :] for r in range(4)], axis=0))[:B]
 
         def clear(p, _):
             acc[p] = jnp.zeros((B, L), F32)
@@ -144,6 +148,7 @@
         grid=(fine // ROWS,),
         out_shape=(
             jax.ShapeDtypeStruct((n_inner * RC * SC * width, L), F32),
+            jax.ShapeDtypeStruct((L, L), F32),
             jax.ShapeDtypeStruct((B, B), F32),
         ),
         in_specs=[
@@ -155,7 +160,7 @@
             smem,
             smem,
         ],
-        out_specs=(vmem, vmem),
+        out_specs=(vmem, vmem, vmem),
         scratch_shapes=[
             pltpu.VMEM((2, width * slots, L), F32),
             pltpu.VMEM((width * fine, L), F32),
@@ -170,24 +175,256 @@
     )(a_blocks, q_blocks, g_level, a_cols, part_of, part_dest, part_pos)
 
 
-def partner_2(shard, axis, stride):
-    return lax.ppermute(shard, axis, [(i, i ^ 1 << stride) for i in range(lax.axis_size(axis))])
+def merge_kernel(
+    n_gx, pieces, dense, h_ref, ht_ref, first_ref, last_ref, own, pair, right, left, half, other, parts, full, done, nat, local_sem,
+    pair_send, pair_recv, right_send, right_recv, left_send, left_recv, core_send, core_recv, part_send, part_recv, full_send, full_recv,
+):
+    gx = lax.axis_index("gx")
+    gy = lax.axis_index("gy")
+    n = own.shape[0]
+    core, z = lax.rem(gy, 2), gy // 2
+    owned = own.shape[1]
+    cell_rows = owned // RC
+    piece = owned // pieces
+    peers = n_gx * 2
+    share = cell_rows // peers
+    rank = gx * 2 + lax.rem(z, 2)
+
+    def remote(src, dst, send, recv, x, y):
+        return pltpu.make_async_remote_copy(
+            src_ref=src, dst_ref=dst, send_sem=send, recv_sem=recv, device_id=(x, y), device_id_type=pl.DeviceIdType.MESH
+        )
+
+    def peer(offset):
+        other_rank = lax.rem(rank + offset, peers)
+        return other_rank, other_rank // 2, (z // 2 * 2 + lax.rem(other_rank, 2)) * 2 + core
+
+    barrier = pltpu.get_barrier_semaphore()
+
+    def greet(x, y):
+        pl.semaphore_signal(barrier, inc=1, device_id=(x, y), device_id_type=pl.DeviceIdType.MESH)
+
+    partner = gy + 1 - 2 * core
+    greet(gx, partner)
+
+    @pl.when(z > 0)
+    def _():
+        greet(gx, gy - 2)
+
+    @pl.when(z < n - 1)
+    def _():
+        greet(gx, gy + 2)
+
+    for offset in range(1, peers):
+        _, x, y = peer(offset)
+        greet(x, y)
+
+    def keep(d):
+        return pltpu.make_async_copy(dense.at[2 * d + core], own.at[d], local_sem.at[d])
+
+    def give(d):
+        return remote(dense.at[2 * d + 1 - core], pair.at[d], pair_send.at[d], pair_recv.at[d], gx, partner)
+
+    order = [d for t in range(n) for d in (n - 1 - t, t)][:n]
+    for d in order:
+        keep(d).start()
+    pl.semaphore_wait(barrier, peers + (z > 0).astype(jnp.int32) + (z < n - 1).astype(jnp.int32))
+    for d in order:
+        give(d).start()
+
+    def go_right(d, c):
+        rows = pl.ds(c * piece, piece)
+        return remote(own.at[d, rows], right.at[d, rows], right_send.at[d, c], right_recv.at[d, c], gx, gy + 2)
+
+    def go_left(d, c):
+        rows = pl.ds(c * piece, piece)
+        return remote(own.at[d, rows], left.at[d, rows], left_send.at[d, c], left_recv.at[d, c], gx, gy - 2)
+
+    def arrive(d):
+        keep(d).wait()
+        give(d).wait_recv()
+
+    def step(s, _):
+        t, c = s // pieces, lax.rem(s, pieces)
+        rows = pl.ds(pl.multiple_of(c * piece, 8), piece)
+        far, near = n - 1 - t, t
+
+        @pl.when(z < far)
+        def _():
+            @pl.when(c == 0)
+            def _():
+                arrive(far)
+
+            own[far, rows] = own[far, rows] + pair[far, rows]
+
+            @pl.when(z > 0)
+            def _():
+                go_right(far, c).wait_recv()
+                own[far, rows] = own[far, rows] + right[far, rows]
+
+            go_right(far, c).start()
+
+        @pl.when(z > near)
+        def _():
+            @pl.when(c == 0)
+            def _():
+                arrive(near)
+
+            own[near, rows] = own[near, rows] + pair[near, rows]
+
+            @pl.when(z < n - 1)
+            def _():
+                go_left(near, c).wait_recv()
+                own[near, rows] = own[near, rows] + left[near, rows]
+
+            go_left(near, c).start()
+
+        return 0
+
+    lax.fori_loop(0, (n - 1) * pieces, step, 0)
+
+    arrive(z)
+    own[z] = own[z] + pair[z]
+
+    @pl.when(z < n - 1)
+    def _():
+        for c in range(pieces):
+            go_left(z, c).wait_recv()
+        own[z] = own[z] + left[z]
+
+    @pl.when(z > 0)
+    def _():
+        for c in range(pieces):
+            go_right(z, c).wait_recv()
+        own[z] = own[z] + right[z]
+
+    mine = pl.ds(pl.multiple_of(core * cell_rows, 8), cell_rows)
+    theirs = pl.ds(pl.multiple_of((1 - core) * cell_rows, 8), cell_rows)
+    swap = remote(own.at[z, theirs], other, core_send.at[0], core_recv.at[0], gx, partner)
+    swap.start()
+    swap.wait_recv()
+    half[...] = own[z, mine] + other[...]
+
+    def scatter(offset):
+        to, x, y = peer(offset)
+        rows = pl.ds(pl.multiple_of(to * share, 8), share)
+        return remote(half.at[rows], parts.at[peers - offset - 1], part_send.at[offset - 1], part_recv.at[peers - offset - 1], x, y)
+
+    def scattered(offset):
+        _, x, y = peer(offset)
+        rows = pl.ds(0, share)
+        return remote(half.at[rows], parts.at[offset - 1], part_send.at[offset - 1], part_recv.at[offset - 1], x, y)
+
+    for offset in range(1, peers):
+        scatter(offset).start()
+
+    for u in range(cell_rows // SC):
+        for r in range(RC):
+            first_ref[r, :, u * L : (u + 1) * L] = own[z, r * cell_rows + u * SC : r * cell_rows + (u + 1) * SC, :]
+
+    here = pl.ds(pl.multiple_of(rank * share, 8), share)
+    total = half[here]
+    for offset in range(1, peers):
+        scattered(offset).wait_recv()
+        total = total + parts[offset - 1]
+    full[here] = total
+
+    def gather(offset):
+        _, x, y = peer(offset)
+        return remote(full.at[here], full.at[here], full_send.at[offset - 1], full_recv.at[peers - offset - 1], x, y)
+
+    def gathered(offset):
+        source, x, y = peer(offset)
+        rows = pl.ds(pl.multiple_of(source * share, 8), share)
+        return remote(full.at[rows], full.at[rows], full_send.at[offset - 1], full_recv.at[offset - 1], x, y)
+
+    for offset in range(1, peers):
+        gather(offset).start()
+    for offset in range(1, peers):
+        gathered(offset).wait_recv()
+
+    blocks = jnp.concatenate([row for s in range(SC) for row in split_rows(tiles(full, s, SC))], axis=0)
+    dot = functools.partial(jnp.dot, precision=lax.Precision.HIGHEST, preferred_element_type=F32)
+    after = dot(blocks, h_ref[...])
+    after = dot(ht_ref[...], jnp.concatenate([after[s * B : (s + 1) * B] for s in range(SC)], axis=1))
+    for s in range(SC):
+        nat[s] = after[:, s * L : (s + 1) * L]
+        flat = join_rows([nat[s, pl.ds(r, G, stride=4), :] for r in range(4)])
+        for m in range(3):
+            done[core, pl.ds(m * SC + s, G, stride=3 * SC), :] = flat[m]
+
+    finish = remote(done.at[core], done.at[core], core_send.at[1], core_recv.at[1], gx, partner)
+    finish.start()
+    finished = remote(done.at[1 - core], done.at[1 - core], core_send.at[1], core_recv.at[1], gx, partner)
+    finished.wait_recv()
+    for u in range(cell_rows // SC):
+        for r in range(RC):
+            last_ref[r, :, u * L : (u + 1) * L] = done[r, u * SC : (u + 1) * SC, :]
+
+    finish.wait_send()
+    swap.wait_send()
+    for offset in range(1, peers):
+        scatter(offset).wait_send()
+        gather(offset).wait_send()
+    for d in range(n):
+        give(d).wait_send()
+
+        @pl.when(z < d)
+        def _():
+            for c in range(pieces):
+                go_right(d, c).wait_send()
+
+        @pl.when(z > d)
+        def _():
+            for c in range(pieces):
+                go_left(d, c).wait_send()
+
+
+def merge(dense, h, ht, n_gx, n_inner, flat):
+    pieces = 4
+    n = n_inner // 2
+    peers = n_gx * 2
+    owned = dense.shape[0] // n_inner
+    cell_rows = owned // RC
+    vmem = pl.BlockSpec(memory_space=pltpu.VMEM)
+    dma = pltpu.SemaphoreType.DMA
+    out = jax.ShapeDtypeStruct((RC, SC, flat), F32)
+    return pl.pallas_call(
+        functools.partial(merge_kernel, n_gx, pieces),
+        out_shape=(out, out),
+        in_specs=[pl.BlockSpec(memory_space=pl.ANY), vmem, vmem],
+        out_specs=(vmem, vmem),
+        scratch_shapes=[pltpu.VMEM((n, owned, L), F32)] * 4
+        + [
+            pltpu.VMEM((cell_rows, L), F32),
+            pltpu.VMEM((cell_rows, L), F32),
+            pltpu.VMEM((peers - 1, cell_rows // peers, L), F32),
+            pltpu.VMEM((cell_rows, L), F32),
+            pltpu.VMEM((RC, cell_rows, L), F32),
+            pltpu.VMEM((SC, B, L), F32),
+            dma((n,)),
+            dma((n,)),
+            dma((n,)),
+            dma((n, pieces)),
+            dma((n, pieces)),
+            dma((n, pieces)),
+            dma((n, pieces)),
+            dma((2,)),
+            dma((2,)),
+            dma((peers - 1,)),
+            dma((peers - 1,)),
+            dma((peers - 1,)),
+            dma((peers - 1,)),
+        ],
+        compiler_params=pltpu.CompilerParams(collective_id=0, has_side_effects=True, vmem_limit_bytes=56 * 2**20),
+        cost_estimate=pl.CostEstimate(flops=4 * RC * SC * B**3, bytes_accessed=dense.size * 4, transcendentals=0),
+    )(dense.reshape(n_inner, owned, L), h, ht)
 
 
 def local(a_blocks, a_cols, q_blocks, part_of, part_dest, part_pos, g_level):
-    flat = a_blocks.shape[2]
-    width = flat // L
-    n_inner = lax.axis_size("gy")
-    dense, h = products(a_blocks, a_cols, q_blocks, part_of, part_dest, part_pos, g_level, n_inner)
-    coarse = lax.psum_scatter(dense, "gy", scatter_dimension=0, tiled=True)
-    first = coarse.reshape(RC, width, SC, L).transpose(0, 2, 1, 3).reshape(RC, SC, flat)
-    total = lax.psum(coarse, "gx")
-    for bit in range(2):
-        total = total + partner_2(total, "gy", bit)
-    total = total.reshape(RC, width, SC, L).transpose(0, 2, 1, 3).reshape(RC * SC, B, B)
-    right = jnp.einsum("mab,bj->maj", total, h, precision=lax.Precision.HIGHEST)
-    last = jnp.einsum("ai,maj->mij", h, right, precision=lax.Precision.HIGHEST)
-    return first, last.reshape(RC, SC, flat)
+    n_gx, n_inner = lax.axis_size("gx"), lax.axis_size("gy")
+    dense, h, ht = products(a_blocks, a_cols, q_blocks, part_of, part_dest, part_pos, g_level, n_inner)
+    return merge(dense, h, ht, n_gx, n_inner, a_blocks.shape[2])
 
 
 def solution(mesh):

time: 192 us -> 128 us (0.67)
  waiting for transfers between devices: 120 us -> 0 us
  Pallas kernels: 44.7 us -> 118 us
  between operations: 14.1 us -> 0.64 us
  matrix products: 2.61 us -> 0 us
  local copies, waits for them, and re-layouts: 5.93 us -> 7.93 us
    pallas_call x0 -> x1, Pallas kernels: none -> 72.7 us  [merge(): pl.pallas_call(functools.partial(merge_kernel, n_gx, pieces), out_shape=(...]
    reduce_scatter x1 -> x0, waiting for transfers between devices: 53.6 us -> none  [local(): coarse = lax.psum_scatter(dense, 'gy', scatter_dimension=0, tiled=True)]
    psum x1 -> x0, waiting for transfers between devices: 50.6 us -> none  [local(): total = lax.psum(coarse, 'gx')]
    ppermute x2 -> x0, waiting for transfers between devices: 16.1 us -> none  [partner_2(): lax.ppermute(shard, axis, [(i, i ^ 1 << stride) for i in range(lax.axis_s...]
    unnamed x5, local copies, waits for them, and re-layouts: 4.12 us -> 7.93 us
    dot_general x2 -> x0, matrix products: 2.61 us -> none  [the longest x1 1.84 us: local(): right = jnp.einsum('mab,bj->maj', total, h, precision=lax.Precision.HIGHEST)]
  transfers between devices with their start and end apart: 4 -> 0, of which waited for: 4 -> 0; matrix products, arithmetic and copies ran while one was open for 0% -> 0% of each run, Pallas kernels for 0% -> 0%
where the time goes in v2:
time: 128 us; the launch traced here: 126 us
  Pallas kernels  118 us (92%)
  local copies, waits for them, and re-layouts  7.93 us (6%)
    pallas_call x1, Pallas kernels, merge(): pl.pallas_call(functools.partial(merge_kernel, n_gx, pieces), out_shape=(...  72.7 us
    pallas_call x1, Pallas kernels, products(): pl.pallas_call(products_kernel, grid=(fine // ROWS,), out_shape=(jax.Shap...  44.9 us
    unnamed x5, local copies, waits for them, and re-layouts  7.93 us

profile of v2, /device:TPU:16, one launch (start us, length us, event | category | flops | bytes accessed | tf_op | source)
XLA Modules:
  0.0 126.2 jit_solution(10915171542996968163)
XLA Ops:
  0.6 1.4 %copy.9.cols_ref = s32[64,8]{1,0:T(8,128)} copy(s32[64,8]{0,1:T(8,128)} %param.8) | data formatting | bytes 4096 | tf_op args[1]
  2.0 1.4 %copy.10.part_ref = s32[64,8]{1,0:T(8,128)} copy(s32[64,8]{0,1:T(8,128)} %param.10) | data formatting | bytes 4096 | tf_op args[3]
  3.4 1.3 %copy.11.dest_ref = s32[64,1]{1,0:T(8,128)} copy(s32[64,1]{0,1:T(1,128)} %param.11) | data formatting | bytes 512 | tf_op args[4]
  4.7 44.9 %shard_map.86 = (f32[9216,128]{1,0:T(8,128)}, f32[128,128]{1,0:T(8,128)}, f32[96,96]{1,0:T(8,128)}) custom-call(bf16[64,8,9216]{2,1,0:T(8,128)(2,1)} %a_ref.1, bf16[64,9216]{1,0:T(8,128)(2,1)} %q_ref.1, f32[3,9216]{1,0:T(4,128)} %g_ref.1, s32[64,8]{1,0:T(8,128)} %copy.9.cols_ref, s32[64,8]{1,0:T(8,128)} %copy.10.part_ref, s32[64,1]{1,0:T(8,128)} %copy.11.dest_ref, ...), custom_call_target="tpu_custom_call" | custom-call | flops 1811939328 | bytes 9437184 | tf_op jit(solution)/shard_map/pallas_call | solution.py:146
  49.6 72.7 %shard_map.87 = (f32[2,8,9216]{2,1,0:T(8,128)}, f32[2,8,9216]{2,1,0:T(8,128)}) custom-call(f32[8,1152,128]{2,1,0:T(8,128)} %bitcast.1, f32[128,128]{1,0:T(8,128)} %get-tuple-element.6.h_ref, f32[96,96]{1,0:T(8,128)} %get-tuple-element.7.ht_ref), custom_call_target="tpu_custom_call" | custom-call | flops 56623104 | bytes 4718592 | tf_op jit(solution)/shard_map/pallas_call | solution.py:392
  122.3 1.9 %copy.14 = f32[2,8,9216]{2,1,0:T(8,128)} copy(f32[2,8,9216]{2,1,0:T(8,128)} %get-tuple-element.10) | data formatting | bytes 1179648
  124.2 1.9 %copy.15 = f32[2,8,9216]{2,1,0:T(8,128)} copy(f32[2,8,9216]{2,1,0:T(8,128)} %get-tuple-element.11) | data formatting | bytes 1179648

commit v3 on v2

--- a/solution.py
+++ b/solution.py
@@ -108,10 +108,10 @@
         made = []
         for k in range(slots):
             block = jnp.concatenate(split_rows(tiles(flat, k, slots)), axis=0).astype(BF16)
-            made.append(jnp.dot(block, q_nat[cols_ref[i, k]], preferred_element_type=F32).astype(BF16))
+            made.append(jnp.dot(block, q_nat[cols_ref[k, i]], preferred_element_type=F32).astype(BF16))
         term = jnp.dot(q_tr[i], jnp.concatenate(made, axis=1), preferred_element_type=F32)
         for k in range(slots):
-            p = part_ref[i, k]
+            p = part_ref[k, i]
             acc[p] += term[:, k * L : (k + 1) * L]
 
     def pair(j, _):
@@ -127,7 +127,7 @@
 
         def one_part(p, _):
             place = pos_ref[p]
-            base = (dest_ref[p, 0] * RC + place // SC) * cell_rows + lax.rem(place, SC)
+            base = (dest_ref[0, p] * RC + place // SC) * cell_rows + lax.rem(place, SC)
             flat = join_rows([acc[p, pl.ds(r, G, stride=4), :] for r in range(4)])
             for m in range(3):
                 where = pl.ds(base + m * SC, G, stride=3 * SC)
@@ -172,12 +172,14 @@
         ],
         compiler_params=pltpu.CompilerParams(dimension_semantics=("arbitrary",), vmem_limit_bytes=56 * 2**20),
         cost_estimate=pl.CostEstimate(flops=4 * fine * slots * B**3, bytes_accessed=a_blocks.size * 2, transcendentals=0),
-    )(a_blocks, q_blocks, g_level, a_cols, part_of, part_dest, part_pos)
+    )(a_blocks, q_blocks, g_level, a_cols.T, part_of.T, part_dest.T, part_pos)
 
 
 def merge_kernel(
-    n_gx, pieces, dense, h_ref, ht_ref, first_ref, last_ref, own, pair, right, left, half, other, parts, full, done, nat, local_sem,
-    pair_send, pair_recv, right_send, right_recv, left_send, left_recv, core_send, core_recv, part_send, part_recv, full_send, full_recv,
+    n_gx, pieces, depth, dense, h_ref, ht_ref, first_ref, last_ref,
+    own, pair, right, left, half, give_half, other, slabs, mixed, parts, full, done, nat,
+    local_sem, pair_send, pair_recv, right_send, right_recv, left_send, left_recv,
+    core_send, core_recv, slab_send, slab_recv, part_send, part_recv, full_send, full_recv,
 ):
     gx = lax.axis_index("gx")
     gy = lax.axis_index("gy")
@@ -207,14 +209,10 @@
     partner = gy + 1 - 2 * core
     greet(gx, partner)
 
-    @pl.when(z > 0)
-    def _():
-        greet(gx, gy - 2)
-
-    @pl.when(z < n - 1)
-    def _():
-        greet(gx, gy + 2)
-
+    for offset in range(1, n):
+        greet(gx, 2 * lax.rem(z + offset, n) + core)
+    for offset in range(1, n_gx):
+        greet(lax.rem(gx + offset, n_gx), gy)
     for offset in range(1, peers):
         _, x, y = peer(offset)
         greet(x, y)
@@ -228,7 +226,7 @@
     order = [d for t in range(n) for d in (n - 1 - t, t)][:n]
     for d in order:
         keep(d).start()
-    pl.semaphore_wait(barrier, peers + (z > 0).astype(jnp.int32) + (z < n - 1).astype(jnp.int32))
+    pl.semaphore_wait(barrier, n + n_gx + peers - 2)
     for d in order:
         give(d).start()
 
@@ -243,48 +241,155 @@
     def arrive(d):
         keep(d).wait()
         give(d).wait_recv()
+        own[d] = own[d] + pair[d]
 
     def step(s, _):
         t, c = s // pieces, lax.rem(s, pieces)
         rows = pl.ds(pl.multiple_of(c * piece, 8), piece)
         far, near = n - 1 - t, t
+        back = s - depth
+        back_t, back_c = jnp.maximum(back, 0) // pieces, lax.rem(jnp.maximum(back, 0), pieces)
+
+        @pl.when((back >= 0) & (z < n - 1 - back_t))
+        def _():
+            go_right(n - 1 - back_t, back_c).wait_send()
+
+        @pl.when((back >= 0) & (z > back_t))
+        def _():
+            go_left(back_t, back_c).wait_send()
 
         @pl.when(z < far)
         def _():
-            @pl.when(c == 0)
-            def _():
-                arrive(far)
-
-            own[far, rows] = own[far, rows] + pair[far, rows]
-
             @pl.when(z > 0)
             def _():
                 go_right(far, c).wait_recv()
                 own[far, rows] = own[far, rows] + right[far, rows]
 
-            go_right(far, c).start()
+            @pl.when((s > 0) | (z > 0))
+            def _():
+                go_right(far, c).start()
 
         @pl.when(z > near)
         def _():
-            @pl.when(c == 0)
-            def _():
-                arrive(near)
-
-            own[near, rows] = own[near, rows] + pair[near, rows]
-
             @pl.when(z < n - 1)
             def _():
                 go_left(near, c).wait_recv()
                 own[near, rows] = own[near, rows] + left[near, rows]
 
-            go_left(near, c).start()
+            @pl.when((s > 0) | (z < n - 1))
+            def _():
+                go_left(near, c).start()
 
         return 0
 
-    lax.fori_loop(0, (n - 1) * pieces, step, 0)
-
-    arrive(z)
-    own[z] = own[z] + pair[z]
+    groups = n // 2
+    mine = pl.ds(pl.multiple_of(core * cell_rows, 8), cell_rows)
+    theirs = pl.ds(pl.multiple_of((1 - core) * cell_rows, 8), cell_rows)
+    swap = remote(give_half, other, core_send.at[0], core_recv.at[0], gx, partner)
+    slab = cell_rows // n_gx
+    here = pl.ds(pl.multiple_of(rank * share, 8), share)
+
+    def group_sums():
+        for g in range(groups):
+            give_half[g] = own[2 * g, theirs] + own[2 * g + 1, theirs]
+        swap.start()
+        for g in range(groups):
+            half[g] = own[2 * g, mine] + own[2 * g + 1, mine]
+
+    def across(offset):
+        to = lax.rem(gx + offset, n_gx)
+        rows = pl.ds(pl.multiple_of(to * slab, 8), slab)
+        at = n_gx - offset - 1
+        return remote(half.at[:, rows], slabs.at[at], slab_send.at[offset - 1], slab_recv.at[at], to, gy)
+
+    def crossed(offset):
+        return remote(slabs.at[offset - 1], slabs.at[offset - 1], slab_send.at[offset - 1], slab_recv.at[offset - 1], gx, partner)
+
+    def spread():
+        swap.wait_recv()
+        half[...] = half[...] + other[...]
+        for offset in range(1, n_gx):
+            across(offset).start()
+
+    def along(offset):
+        to = lax.rem(z + offset, n)
+        rows = pl.ds(pl.multiple_of(lax.rem(to, 2) * share, 8), share)
+        at = n - offset - 1
+        return remote(mixed.at[to // 2, rows], parts.at[at], part_send.at[offset - 1], part_recv.at[at], gx, 2 * to + core)
+
+    def went(offset):
+        return remote(parts.at[offset - 1], parts.at[offset - 1], part_send.at[offset - 1], part_recv.at[offset - 1], gx, partner)
+
+    def descend():
+        total = half[:, pl.ds(pl.multiple_of(gx * slab, 8), slab)]
+        for offset in range(1, n_gx):
+            crossed(offset).wait_recv()
+            total = total + slabs[offset - 1]
+        mixed[...] = total
+        for offset in range(1, n):
+            along(offset).start()
+
+    def gather(offset):
+        _, x, y = peer(offset)
+        return remote(full.at[here], full.at[here], full_send.at[offset - 1], full_recv.at[peers - offset - 1], x, y)
+
+    def gathered(offset):
+        source, x, y = peer(offset)
+        rows = pl.ds(pl.multiple_of(source * share, 8), share)
+        return remote(full.at[rows], full.at[rows], full_send.at[offset - 1], full_recv.at[offset - 1], x, y)
+
+    def collect():
+        total = mixed[z // 2, pl.ds(pl.multiple_of(lax.rem(z, 2) * share, 8), share)]
+        for offset in range(1, n):
+            went(offset).wait_recv()
+            total = total + parts[offset - 1]
+        full[here] = total
+        for offset in range(1, peers):
+            gather(offset).start()
+
+    finish = remote(done.at[core], done.at[core], core_send.at[1], core_recv.at[1], gx, partner)
+    finished = remote(done.at[1 - core], done.at[1 - core], core_send.at[1], core_recv.at[1], gx, partner)
+
+    def project():
+        for offset in range(1, peers):
+            gathered(offset).wait_recv()
+        blocks = jnp.concatenate([row for s in range(SC) for row in split_rows(tiles(full, s, SC))], axis=0)
+        dot = functools.partial(jnp.dot, precision=lax.Precision.HIGHEST, preferred_element_type=F32)
+        after = dot(blocks, h_ref[...])
+        after = dot(ht_ref[...], jnp.concatenate([after[s * B : (s + 1) * B] for s in range(SC)], axis=1))
+        for s in range(SC):
+            nat[s] = after[:, s * L : (s + 1) * L]
+            flat = join_rows([nat[s, pl.ds(r, G, stride=4), :] for r in range(4)])
+            for m in range(3):
+                done[core, pl.ds(m * SC + s, G, stride=3 * SC), :] = flat[m]
+        finish.start()
+
+    def write_last():
+        finished.wait_recv()
+        for u in range(cell_rows // SC):
+            for r in range(RC):
+                last_ref[r, :, u * L : (u + 1) * L] = done[r, u * SC : (u + 1) * SC, :]
+
+    steps = (n - 1) * pieces
+    arrive(n - 1)
+
+    @pl.when(z == 0)
+    def _():
+        go_right(n - 1, 0).start()
+
+    arrive(0)
+
+    @pl.when(z == n - 1)
+    def _():
+        go_left(0, 0).start()
+
+    for d in range(1, n - 1):
+        arrive(d)
+    at = 0
+    for stage, stop in ((group_sums, 2), (spread, 4), (descend, 6), (collect, 8), (project, 10), (write_last, steps)):
+        stage()
+        lax.fori_loop(at, stop, step, 0)
+        at = stop
 
     @pl.when(z < n - 1)
     def _():
@@ -298,90 +403,34 @@
             go_right(z, c).wait_recv()
         own[z] = own[z] + right[z]
 
-    mine = pl.ds(pl.multiple_of(core * cell_rows, 8), cell_rows)
-    theirs = pl.ds(pl.multiple_of((1 - core) * cell_rows, 8), cell_rows)
-    swap = remote(own.at[z, theirs], other, core_send.at[0], core_recv.at[0], gx, partner)
-    swap.start()
-    swap.wait_recv()
-    half[...] = own[z, mine] + other[...]
-
-    def scatter(offset):
-        to, x, y = peer(offset)
-        rows = pl.ds(pl.multiple_of(to * share, 8), share)
-        return remote(half.at[rows], parts.at[peers - offset - 1], part_send.at[offset - 1], part_recv.at[peers - offset - 1], x, y)
-
-    def scattered(offset):
-        _, x, y = peer(offset)
-        rows = pl.ds(0, share)
-        return remote(half.at[rows], parts.at[offset - 1], part_send.at[offset - 1], part_recv.at[offset - 1], x, y)
-
-    for offset in range(1, peers):
-        scatter(offset).start()
-
     for u in range(cell_rows // SC):
         for r in range(RC):
             first_ref[r, :, u * L : (u + 1) * L] = own[z, r * cell_rows + u * SC : r * cell_rows + (u + 1) * SC, :]
 
-    here = pl.ds(pl.multiple_of(rank * share, 8), share)
-    total = half[here]
-    for offset in range(1, peers):
-        scattered(offset).wait_recv()
-        total = total + parts[offset - 1]
-    full[here] = total
-
-    def gather(offset):
-        _, x, y = peer(offset)
-        return remote(full.at[here], full.at[here], full_send.at[offset - 1], full_recv.at[peers - offset - 1], x, y)
-
-    def gathered(offset):
-        source, x, y = peer(offset)
-        rows = pl.ds(pl.multiple_of(source * share, 8), share)
-        return remote(full.at[rows], full.at[rows], full_send.at[offset - 1], full_recv.at[offset - 1], x, y)
-
-    for offset in range(1, peers):
-        gather(offset).start()
-    for offset in range(1, peers):
-        gathered(offset).wait_recv()
-
-    blocks = jnp.concatenate([row for s in range(SC) for row in split_rows(tiles(full, s, SC))], axis=0)
-    dot = functools.partial(jnp.dot, precision=lax.Precision.HIGHEST, preferred_element_type=F32)
-    after = dot(blocks, h_ref[...])
-    after = dot(ht_ref[...], jnp.concatenate([after[s * B : (s + 1) * B] for s in range(SC)], axis=1))
-    for s in range(SC):
-        nat[s] = after[:, s * L : (s + 1) * L]
-        flat = join_rows([nat[s, pl.ds(r, G, stride=4), :] for r in range(4)])
-        for m in range(3):
-            done[core, pl.ds(m * SC + s, G, stride=3 * SC), :] = flat[m]
-
-    finish = remote(done.at[core], done.at[core], core_send.at[1], core_recv.at[1], gx, partner)
-    finish.start()
-    finished = remote(done.at[1 - core], done.at[1 - core], core_send.at[1], core_recv.at[1], gx, partner)
-    finished.wait_recv()
-    for u in range(cell_rows // SC):
-        for r in range(RC):
-            last_ref[r, :, u * L : (u + 1) * L] = done[r, u * SC : (u + 1) * SC, :]
-
     finish.wait_send()
     swap.wait_send()
+    for offset in range(1, n_gx):
+        across(offset).wait_send()
+    for offset in range(1, n):
+        along(offset).wait_send()
     for offset in range(1, peers):
-        scatter(offset).wait_send()
         gather(offset).wait_send()
     for d in range(n):
         give(d).wait_send()
-
-        @pl.when(z < d)
+    for s in range(max(steps - depth, 0), steps):
+        t, c = s // pieces, s % pieces
+
+        @pl.when(z < n - 1 - t)
         def _():
-            for c in range(pieces):
-                go_right(d, c).wait_send()
-
-        @pl.when(z > d)
+            go_right(n - 1 - t, c).wait_send()
+
+        @pl.when(z > t)
         def _():
-            for c in range(pieces):
-                go_left(d, c).wait_send()
+            go_left(t, c).wait_send()
 
 
 def merge(dense, h, ht, n_gx, n_inner, flat):
-    pieces = 4
+    pieces, depth = 4, 2
     n = n_inner // 2
     peers = n_gx * 2
     owned = dense.shape[0] // n_inner
@@ -390,15 +439,18 @@
     dma = pltpu.SemaphoreType.DMA
     out = jax.ShapeDtypeStruct((RC, SC, flat), F32)
     return pl.pallas_call(
-        functools.partial(merge_kernel, n_gx, pieces),
+        functools.partial(merge_kernel, n_gx, pieces, depth),
         out_shape=(out, out),
         in_specs=[pl.BlockSpec(memory_space=pl.ANY), vmem, vmem],
         out_specs=(vmem, vmem),
         scratch_shapes=[pltpu.VMEM((n, owned, L), F32)] * 4
         + [
-            pltpu.VMEM((cell_rows, L), F32),
-            pltpu.VMEM((cell_rows, L), F32),
-            pltpu.VMEM((peers - 1, cell_rows // peers, L), F32),
+            pltpu.VMEM((n // 2, cell_rows, L), F32),
+            pltpu.VMEM((n // 2, cell_rows, L), F32),
+            pltpu.VMEM((n // 2, cell_rows, L), F32),
+            pltpu.VMEM((n_gx - 1, n // 2, cell_rows // n_gx, L), F32),
+            pltpu.VMEM((n // 2, cell_rows // n_gx, L), F32),
+            pltpu.VMEM((n - 1, cell_rows // peers, L), F32),
             pltpu.VMEM((cell_rows, L), F32),
             pltpu.VMEM((RC, cell_rows, L), F32),
             pltpu.VMEM((SC, B, L), F32),
@@ -411,8 +463,10 @@
             dma((n, pieces)),
             dma((2,)),
             dma((2,)),
-            dma((peers - 1,)),
-            dma((peers - 1,)),
+            dma((n_gx - 1,)),
+            dma((n_gx - 1,)),
+            dma((n - 1,)),
+            dma((n - 1,)),
             dma((peers - 1,)),
             dma((peers - 1,)),
         ],

time: 128 us -> 123 us (0.961)
  local copies, waits for them, and re-layouts: 7.93 us -> 3.83 us
    unnamed x5 -> x2, local copies, waits for them, and re-layouts: 7.93 us -> 3.83 us
where the time goes in v3:
time: 123 us; the launch traced here: 122 us
  Pallas kernels  117 us (95%)
  local copies, waits for them, and re-layouts  3.83 us (3%)
    pallas_call x1, Pallas kernels, merge(): pl.pallas_call(functools.partial(merge_kernel, n_gx, pieces, depth), out_...  73.2 us
    pallas_call x1, Pallas kernels, products(): pl.pallas_call(products_kernel, grid=(fine // ROWS,), out_shape=(jax.Shap...  44.1 us
    unnamed x2, local copies, waits for them, and re-layouts  3.83 us

profile of v3, /device:TPU:16, one launch (start us, length us, event | category | flops | bytes accessed | tf_op | source)
XLA Modules:
  0.0 121.7 jit_solution(14184529824631654445)
XLA Ops:
  0.6 44.1 %shard_map.86 = (f32[9216,128]{1,0:T(8,128)}, f32[128,128]{1,0:T(8,128)}, f32[96,96]{1,0:T(8,128)}) custom-call(bf16[64,8,9216]{2,1,0:T(8,128)(2,1)} %a_ref.1, bf16[64,9216]{1,0:T(8,128)(2,1)} %q_ref.1, f32[3,9216]{1,0:T(4,128)} %g_ref.1, s32[8,64]{1,0:T(8,128)} %bitcast.5, s32[8,64]{1,0:T(8,128)} %bitcast.6, s32[1,64]{1,0:T(1,128)} %bitcast.7, s32[64]{0:T(128)} %pos_ref.1), custom_call_target="tpu_custom_call" | custom-call | flops 1811939328 | bytes 9437184 | tf_op jit(solution)/shard_map/pallas_call | solution.py:146
  44.7 73.2 %shard_map.87 = (f32[2,8,9216]{2,1,0:T(8,128)}, f32[2,8,9216]{2,1,0:T(8,128)}) custom-call(f32[8,1152,128]{2,1,0:T(8,128)} %bitcast.4, f32[128,128]{1,0:T(8,128)} %get-tuple-element.6.h_ref, f32[96,96]{1,0:T(8,128)} %get-tuple-element.7.ht_ref), custom_call_target="tpu_custom_call" | custom-call | flops 56623104 | bytes 4718592 | tf_op jit(solution)/shard_map/pallas_call | solution.py:441
  117.9 1.9 %copy.11 = f32[2,8,9216]{2,1,0:T(8,128)} copy(f32[2,8,9216]{2,1,0:T(8,128)} %get-tuple-element.10) | data formatting | bytes 1179648
  119.8 1.9 %copy.12 = f32[2,8,9216]{2,1,0:T(8,128)} copy(f32[2,8,9216]{2,1,0:T(8,128)} %get-tuple-element.11) | data formatting | bytes 1179648

commit v4 on v3

--- a/solution.py
+++ b/solution.py
@@ -197,10 +197,6 @@
             src_ref=src, dst_ref=dst, send_sem=send, recv_sem=recv, device_id=(x, y), device_id_type=pl.DeviceIdType.MESH
         )
 
-    def peer(offset):
-        other_rank = lax.rem(rank + offset, peers)
-        return other_rank, other_rank // 2, (z // 2 * 2 + lax.rem(other_rank, 2)) * 2 + core
-
     barrier = pltpu.get_barrier_semaphore()
 
     def greet(x, y):
@@ -213,9 +209,6 @@
         greet(gx, 2 * lax.rem(z + offset, n) + core)
     for offset in range(1, n_gx):
         greet(lax.rem(gx + offset, n_gx), gy)
-    for offset in range(1, peers):
-        _, x, y = peer(offset)
-        greet(x, y)
 
     def keep(d):
         return pltpu.make_async_copy(dense.at[2 * d + core], own.at[d], local_sem.at[d])
@@ -226,7 +219,7 @@
     order = [d for t in range(n) for d in (n - 1 - t, t)][:n]
     for d in order:
         keep(d).start()
-    pl.semaphore_wait(barrier, n + n_gx + peers - 2)
+    pl.semaphore_wait(barrier, n + n_gx - 1)
     for d in order:
         give(d).start()
 
@@ -329,14 +322,19 @@
         for offset in range(1, n):
             along(offset).start()
 
+    twin = gy + 2 - 4 * lax.rem(z, 2)
+    slab_rows = pl.ds(pl.multiple_of(gx * slab, 8), slab)
+    pass_on = remote(full.at[here], full.at[here], core_send.at[2], core_recv.at[2], gx, twin)
+
     def gather(offset):
-        _, x, y = peer(offset)
-        return remote(full.at[here], full.at[here], full_send.at[offset - 1], full_recv.at[peers - offset - 1], x, y)
+        to = lax.rem(gx + offset, n_gx)
+        at = n_gx - offset - 1
+        return remote(full.at[slab_rows], full.at[slab_rows], full_send.at[offset - 1], full_recv.at[at], to, gy)
 
     def gathered(offset):
-        source, x, y = peer(offset)
-        rows = pl.ds(pl.multiple_of(source * share, 8), share)
-        return remote(full.at[rows], full.at[rows], full_send.at[offset - 1], full_recv.at[offset - 1], x, y)
+        source = lax.rem(gx + offset, n_gx)
+        rows = pl.ds(pl.multiple_of(source * slab, 8), slab)
+        return remote(full.at[rows], full.at[rows], full_send.at[offset - 1], full_recv.at[offset - 1], source, gy)
 
     def collect():
         total = mixed[z // 2, pl.ds(pl.multiple_of(lax.rem(z, 2) * share, 8), share)]
@@ -344,14 +342,20 @@
             went(offset).wait_recv()
             total = total + parts[offset - 1]
         full[here] = total
-        for offset in range(1, peers):
+        pass_on.start()
+
+    def fan_out():
+        other_rank = rank + 1 - 2 * lax.rem(rank, 2)
+        rows = pl.ds(pl.multiple_of(other_rank * share, 8), share)
+        remote(full.at[rows], full.at[rows], core_send.at[2], core_recv.at[2], gx, twin).wait_recv()
+        for offset in range(1, n_gx):
             gather(offset).start()
 
     finish = remote(done.at[core], done.at[core], core_send.at[1], core_recv.at[1], gx, partner)
     finished = remote(done.at[1 - core], done.at[1 - core], core_send.at[1], core_recv.at[1], gx, partner)
 
     def project():
-        for offset in range(1, peers):
+        for offset in range(1, n_gx):
             gathered(offset).wait_recv()
         blocks = jnp.concatenate([row for s in range(SC) for row in split_rows(tiles(full, s, SC))], axis=0)
         dot = functools.partial(jnp.dot, precision=lax.Precision.HIGHEST, preferred_element_type=F32)
@@ -385,9 +389,20 @@
 
     for d in range(1, n - 1):
         arrive(d)
+    edge = (z == 0) | (z == n - 1)
+    busy = steps - pieces
     at = 0
-    for stage, stop in ((group_sums, 2), (spread, 4), (descend, 6), (collect, 8), (project, 10), (write_last, steps)):
+    for stage, at_edge, between in (
+        (group_sums, 2, 0),
+        (spread, 4, 0),
+        (descend, 6, 1),
+        (collect, 7, 3),
+        (fan_out, 9, busy),
+        (project, 10, busy),
+        (write_last, steps, steps),
+    ):
         stage()
+        stop = jnp.where(edge, at_edge, between)
         lax.fori_loop(at, stop, step, 0)
         at = stop
 
@@ -413,7 +428,8 @@
         across(offset).wait_send()
     for offset in range(1, n):
         along(offset).wait_send()
-    for offset in range(1, peers):
+    pass_on.wait_send()
+    for offset in range(1, n_gx):
         gather(offset).wait_send()
     for d in range(n):
         give(d).wait_send()
@@ -430,7 +446,7 @@
 
 
 def merge(dense, h, ht, n_gx, n_inner, flat):
-    pieces, depth = 4, 2
+    pieces, depth = 4, 4
     n = n_inner // 2
     peers = n_gx * 2
     owned = dense.shape[0] // n_inner
@@ -461,14 +477,14 @@
             dma((n, pieces)),
             dma((n, pieces)),
             dma((n, pieces)),
-            dma((2,)),
-            dma((2,)),
+            dma((3,)),
+            dma((3,)),
             dma((n_gx - 1,)),
             dma((n_gx - 1,)),
             dma((n - 1,)),
             dma((n - 1,)),
-            dma((peers - 1,)),
-            dma((peers - 1,)),
+            dma((n_gx - 1,)),
+            dma((n_gx - 1,)),
         ],
         compiler_params=pltpu.CompilerParams(collective_id=0, has_side_effects=True, vmem_limit_bytes=56 * 2**20),
         cost_estimate=pl.CostEstimate(flops=4 * RC * SC * B**3, bytes_accessed=dense.size * 4, transcendentals=0),

time: 123 us -> 116 us (0.943)
  Pallas kernels: 117 us -> 111 us
    pallas_call x1, Pallas kernels: 73.2 us -> 66.9 us  [merge(): pl.pallas_call(functools.partial(merge_kernel, n_gx, pieces, depth), out_...]
where the time goes in v4:
time: 116 us; the launch traced here: 115 us
  Pallas kernels  111 us (96%)
  local copies, waits for them, and re-layouts  3.83 us (3%)
    pallas_call x1, Pallas kernels, merge(): pl.pallas_call(functools.partial(merge_kernel, n_gx, pieces, depth), out_...  66.9 us
    pallas_call x1, Pallas kernels, products(): pl.pallas_call(products_kernel, grid=(fine // ROWS,), out_shape=(jax.Shap...  44.1 us
    unnamed x2, local copies, waits for them, and re-layouts  3.83 us

profile of v4, /device:TPU:16, one launch (start us, length us, event | category | flops | bytes accessed | tf_op | source)
XLA Modules:
  0.0 115.4 jit_solution(9508584691105379522)
XLA Ops:
  0.6 44.1 %shard_map.86 = (f32[9216,128]{1,0:T(8,128)}, f32[128,128]{1,0:T(8,128)}, f32[96,96]{1,0:T(8,128)}) custom-call(bf16[64,8,9216]{2,1,0:T(8,128)(2,1)} %a_ref.1, bf16[64,9216]{1,0:T(8,128)(2,1)} %q_ref.1, f32[3,9216]{1,0:T(4,128)} %g_ref.1, s32[8,64]{1,0:T(8,128)} %bitcast.5, s32[8,64]{1,0:T(8,128)} %bitcast.6, s32[1,64]{1,0:T(1,128)} %bitcast.7, s32[64]{0:T(128)} %pos_ref.1), custom_call_target="tpu_custom_call" | custom-call | flops 1811939328 | bytes 9437184 | tf_op jit(solution)/shard_map/pallas_call | solution.py:146
  44.7 66.9 %shard_map.87 = (f32[2,8,9216]{2,1,0:T(8,128)}, f32[2,8,9216]{2,1,0:T(8,128)}) custom-call(f32[8,1152,128]{2,1,0:T(8,128)} %bitcast.4, f32[128,128]{1,0:T(8,128)} %get-tuple-element.6.h_ref, f32[96,96]{1,0:T(8,128)} %get-tuple-element.7.ht_ref), custom_call_target="tpu_custom_call" | custom-call | flops 56623104 | bytes 4718592 | tf_op jit(solution)/shard_map/pallas_call | solution.py:457
  111.5 1.9 %copy.11 = f32[2,8,9216]{2,1,0:T(8,128)} copy(f32[2,8,9216]{2,1,0:T(8,128)} %get-tuple-element.10) | data formatting | bytes 1179648
  113.5 1.9 %copy.12 = f32[2,8,9216]{2,1,0:T(8,128)} copy(f32[2,8,9216]{2,1,0:T(8,128)} %get-tuple-element.11) | data formatting | bytes 1179648

commit v5 on v4

--- a/solution.py
+++ b/solution.py
@@ -231,6 +231,14 @@
         rows = pl.ds(c * piece, piece)
         return remote(own.at[d, rows], left.at[d, rows], left_send.at[d, c], left_recv.at[d, c], gx, gy - 2)
 
+    def end_right(c):
+        rows = pl.ds(c * piece, piece)
+        return remote(own.at[n - 1, rows], left.at[n - 1, rows], right_send.at[n - 1, c], left_recv.at[n - 1, c], gx, 2 * (n - 1) + core)
+
+    def end_left(c):
+        rows = pl.ds(c * piece, piece)
+        return remote(own.at[0, rows], right.at[0, rows], left_send.at[0, c], right_recv.at[0, c], gx, core)
+
     def arrive(d):
         keep(d).wait()
         give(d).wait_recv()
@@ -253,25 +261,33 @@
 
         @pl.when(z < far)
         def _():
-            @pl.when(z > 0)
+            @pl.when((z > 1) | ((z > 0) & (t > 0)))
             def _():
                 go_right(far, c).wait_recv()
                 own[far, rows] = own[far, rows] + right[far, rows]
 
-            @pl.when((s > 0) | (z > 0))
+            @pl.when((t > 0) | (z > 0))
             def _():
                 go_right(far, c).start()
 
+            @pl.when((t == 0) & (s > 0) & (z == 0))
+            def _():
+                end_right(c).start()
+
         @pl.when(z > near)
         def _():
-            @pl.when(z < n - 1)
+            @pl.when((z < n - 2) | ((z < n - 1) & (t > 0)))
             def _():
                 go_left(near, c).wait_recv()
                 own[near, rows] = own[near, rows] + left[near, rows]
 
-            @pl.when((s > 0) | (z < n - 1))
+            @pl.when((t > 0) | (z < n - 1))
             def _():
                 go_left(near, c).start()
+
+            @pl.when((t == 0) & (s > 0) & (z == n - 1))
+            def _():
+                end_left(c).start()
 
         return 0
 
@@ -379,13 +395,13 @@
 
     @pl.when(z == 0)
     def _():
-        go_right(n - 1, 0).start()
+        end_right(0).start()
 
     arrive(0)
 
     @pl.when(z == n - 1)
     def _():
-        go_left(0, 0).start()
+        end_left(0).start()
 
     for d in range(1, n - 1):
         arrive(d)
@@ -406,17 +422,10 @@
         lax.fori_loop(at, stop, step, 0)
         at = stop
 
-    @pl.when(z < n - 1)
-    def _():
-        for c in range(pieces):
-            go_left(z, c).wait_recv()
-        own[z] = own[z] + left[z]
-
-    @pl.when(z > 0)
-    def _():
-        for c in range(pieces):
-            go_right(z, c).wait_recv()
-        own[z] = own[z] + right[z]
+    for c in range(pieces):
+        go_left(z, c).wait_recv()
+        go_right(z, c).wait_recv()
+    own[z] = own[z] + left[z] + right[z]
 
     for u in range(cell_rows // SC):
         for r in range(RC):

time: 116 us -> 119 us (1.026)
  Pallas kernels: 111 us -> 114 us
    pallas_call x1, Pallas kernels: 66.9 us -> 70 us  [merge(): pl.pallas_call(functools.partial(merge_kernel, n_gx, pieces, depth), out_...]
where the time goes in v5:
time: 119 us
  Pallas kernels  114 us (96%)
  local copies, waits for them, and re-layouts  3.83 us (3%)
    pallas_call x1, Pallas kernels, merge(): pl.pallas_call(functools.partial(merge_kernel, n_gx, pieces, depth), out_...  70 us
    pallas_call x1, Pallas kernels, products(): pl.pallas_call(products_kernel, grid=(fine // ROWS,), out_shape=(jax.Shap...  44.1 us
    unnamed x2, local copies, waits for them, and re-layouts  3.83 us

profile of v5, /device:TPU:16, one launch (start us, length us, event | category | flops | bytes accessed | tf_op | source)
XLA Modules:
  0.0 118.5 jit_solution(2960599265149149259)
XLA Ops:
  0.6 44.1 %shard_map.86 = (f32[9216,128]{1,0:T(8,128)}, f32[128,128]{1,0:T(8,128)}, f32[96,96]{1,0:T(8,128)}) custom-call(bf16[64,8,9216]{2,1,0:T(8,128)(2,1)} %a_ref.1, bf16[64,9216]{1,0:T(8,128)(2,1)} %q_ref.1, f32[3,9216]{1,0:T(4,128)} %g_ref.1, s32[8,64]{1,0:T(8,128)} %bitcast.5, s32[8,64]{1,0:T(8,128)} %bitcast.6, s32[1,64]{1,0:T(1,128)} %bitcast.7, s32[64]{0:T(128)} %pos_ref.1), custom_call_target="tpu_custom_call" | custom-call | flops 1811939328 | bytes 9437184 | tf_op jit(solution)/shard_map/pallas_call | solution.py:146
  44.7 70.0 %shard_map.87 = (f32[2,8,9216]{2,1,0:T(8,128)}, f32[2,8,9216]{2,1,0:T(8,128)}) custom-call(f32[8,1152,128]{2,1,0:T(8,128)} %bitcast.4, f32[128,128]{1,0:T(8,128)} %get-tuple-element.6.h_ref, f32[96,96]{1,0:T(8,128)} %get-tuple-element.7.ht_ref), custom_call_target="tpu_custom_call" | custom-call | flops 56623104 | bytes 4718592 | tf_op jit(solution)/shard_map/pallas_call | solution.py:466
  114.7 1.9 %copy.11 = f32[2,8,9216]{2,1,0:T(8,128)} copy(f32[2,8,9216]{2,1,0:T(8,128)} %get-tuple-element.10) | data formatting | bytes 1179648
  116.6 1.9 %copy.12 = f32[2,8,9216]{2,1,0:T(8,128)} copy(f32[2,8,9216]{2,1,0:T(8,128)} %get-tuple-element.11) | data formatting | bytes 1179648

commit v6 on v4

--- a/solution.py
+++ b/solution.py
@@ -13,6 +13,7 @@
 RC = 2
 SC = 8
 ROWS = 8
+UNROLL = 4
 F32 = jnp.float32
 BF16 = jnp.bfloat16
 
@@ -64,29 +65,30 @@
         keep = lax.broadcasted_iota(jnp.int32, (B, L), 1) < B
         q_nat[:, B:, :] = jnp.zeros((fine, L - B, L), BF16)
 
-        def one_q(i, _):
-            rows = split_rows(tiles(q_flat, i, fine))
-            for r in range(4):
-                nat[pl.ds(r, G, stride=4), :] = rows[r]
-            q_nat[i, :B, :] = jnp.where(keep, nat[...], 0.0).astype(BF16)
-            permuted = jnp.concatenate(rows, axis=0)
-            q_tr[i] = jnp.transpose(permuted)[:B].astype(BF16)
+        def some_q(j, _):
+            for e in range(UNROLL):
+                rows = split_rows(tiles(q_flat, UNROLL * j + e, fine))
+                for r in range(4):
+                    nat[e, pl.ds(r, G, stride=4), :] = rows[r]
+                q_tr[UNROLL * j + e] = jnp.transpose(jnp.concatenate(rows, axis=0))[:B].astype(BF16)
+            for e in range(UNROLL):
+                q_nat[UNROLL * j + e, :B, :] = jnp.where(keep, nat[e], 0.0).astype(BF16)
             return 0
 
-        lax.fori_loop(0, fine, one_q, 0)
+        lax.fori_loop(0, fine // UNROLL, some_q, 0)
 
         mats = []
         for l in range(3):
             rows = split_rows(tiles(g_flat, l, 8))
             for r in range(4):
-                nat[pl.ds(r, G, stride=4), :] = rows[r]
-            mats.append(nat[...][:, :B])
+                nat[0, pl.ds(r, G, stride=4), :] = rows[r]
+            mats.append(nat[0][:, :B])
         h = jnp.dot(mats[0], mats[1], precision=lax.Precision.HIGHEST, preferred_element_type=F32)
         h = jnp.dot(h, mats[2], precision=lax.Precision.HIGHEST, preferred_element_type=F32)
         h_ref[...] = jnp.zeros((L, L), F32)
         h_ref[:B, :B] = h
-        nat[:, :B] = h
-        ht_ref[...] = jnp.transpose(jnp.concatenate([nat[pl.ds(r, G, stride=4), :] for r in range(4)], axis=0))[:B]
+        nat[0, :, :B] = h
+        ht_ref[...] = jnp.transpose(jnp.concatenate([nat[0, pl.ds(r, G, stride=4), :] for r in range(4)], axis=0))[:B]
 
         def clear(p, _):
             acc[p] = jnp.zeros((B, L), F32)
@@ -100,41 +102,40 @@
 
         lax.fori_loop(0, dense_ref.shape[0] // 128, clear_dense, 0)
 
-    def one_row(rr, slot):
-        i = step * ROWS + rr
-        flat = a_flat.at[slot]
-        for u in range(width):
-            flat[u * slots : (u + 1) * slots, :] = a_ref[rr, :, u * L : (u + 1) * L].astype(F32)
-        made = []
-        for k in range(slots):
-            block = jnp.concatenate(split_rows(tiles(flat, k, slots)), axis=0).astype(BF16)
-            made.append(jnp.dot(block, q_nat[cols_ref[k, i]], preferred_element_type=F32).astype(BF16))
-        term = jnp.dot(q_tr[i], jnp.concatenate(made, axis=1), preferred_element_type=F32)
-        for k in range(slots):
-            p = part_ref[k, i]
-            acc[p] += term[:, k * L : (k + 1) * L]
-
-    def pair(j, _):
-        one_row(2 * j, 0)
-        one_row(2 * j + 1, 1)
+    def some_rows(j, _):
+        for e in range(UNROLL):
+            for u in range(width):
+                a_flat[e, u * slots : (u + 1) * slots, :] = a_ref[UNROLL * j + e, :, u * L : (u + 1) * L].astype(F32)
+        for e in range(UNROLL):
+            i = step * ROWS + UNROLL * j + e
+            made = []
+            for k in range(slots):
+                block = jnp.concatenate(split_rows(tiles(a_flat.at[e], k, slots)), axis=0).astype(BF16)
+                made.append(jnp.dot(block, q_nat[cols_ref[k, i]], preferred_element_type=F32).astype(BF16))
+            term = jnp.dot(q_tr[i], jnp.concatenate(made, axis=1), preferred_element_type=F32)
+            for k in range(slots):
+                p = part_ref[k, i]
+                acc[p] += term[:, k * L : (k + 1) * L]
         return 0
 
-    lax.fori_loop(0, ROWS // 2, pair, 0)
+    lax.fori_loop(0, ROWS // UNROLL, some_rows, 0)
 
     @pl.when(step == pl.num_programs(0) - 1)
     def _():
         cell_rows = width * SC
 
-        def one_part(p, _):
-            place = pos_ref[p]
-            base = (dest_ref[0, p] * RC + place // SC) * cell_rows + lax.rem(place, SC)
-            flat = join_rows([acc[p, pl.ds(r, G, stride=4), :] for r in range(4)])
-            for m in range(3):
-                where = pl.ds(base + m * SC, G, stride=3 * SC)
-                dense_ref[where, :] = dense_ref[where, :] + flat[m]
+        def some_parts(j, _):
+            flats = [join_rows([acc[UNROLL * j + e, pl.ds(r, G, stride=4), :] for r in range(4)]) for e in range(UNROLL)]
+            for e in range(UNROLL):
+                p = UNROLL * j + e
+                place = pos_ref[p]
+                base = (dest_ref[0, p] * RC + place // SC) * cell_rows + lax.rem(place, SC)
+                for m in range(3):
+                    where = pl.ds(base + m * SC, G, stride=3 * SC)
+                    dense_ref[where, :] = dense_ref[where, :] + flats[e][m]
             return 0
 
-        lax.fori_loop(0, n_part, one_part, 0)
+        lax.fori_loop(0, n_part // UNROLL, some_parts, 0)
 
 
 def products(a_blocks, a_cols, q_blocks, part_of, part_dest, part_pos, g_level, n_inner):
@@ -162,10 +163,10 @@
         ],
         out_specs=(vmem, vmem, vmem),
         scratch_shapes=[
-            pltpu.VMEM((2, width * slots, L), F32),
+            pltpu.VMEM((UNROLL, width * slots, L), F32),
             pltpu.VMEM((width * fine, L), F32),
             pltpu.VMEM((width * 8, L), F32),
-            pltpu.VMEM((B, L), F32),
+            pltpu.VMEM((UNROLL, B, L), F32),
             pltpu.VMEM((fine, L, L), BF16),
             pltpu.VMEM((fine, B, B), BF16),
             pltpu.VMEM((n_part, B, L), F32),
@@ -491,10 +492,33 @@
     )(dense.reshape(n_inner, owned, L), h, ht)
 
 
+def hand_over_kernel(first_in, last_in, first_ref, last_ref, sems):
+    copies = []
+    for r in range(RC):
+        copies.append(pltpu.make_async_copy(first_in.at[r], first_ref.at[r], sems.at[0, r]))
+        copies.append(pltpu.make_async_copy(last_in.at[r], last_ref.at[r], sems.at[1, r]))
+    for copy in copies:
+        copy.start()
+    for copy in copies:
+        copy.wait()
+
+
+def hand_over(first, last):
+    anywhere = pl.BlockSpec(memory_space=pl.ANY)
+    return pl.pallas_call(
+        hand_over_kernel,
+        out_shape=(jax.ShapeDtypeStruct(first.shape, F32), jax.ShapeDtypeStruct(last.shape, F32)),
+        in_specs=[anywhere, anywhere],
+        out_specs=(anywhere, anywhere),
+        scratch_shapes=[pltpu.SemaphoreType.DMA((2, RC))],
+        compiler_params=pltpu.CompilerParams(vmem_limit_bytes=56 * 2**20),
+    )(first, last)
+
+
 def local(a_blocks, a_cols, q_blocks, part_of, part_dest, part_pos, g_level):
     n_gx, n_inner = lax.axis_size("gx"), lax.axis_size("gy")
     dense, h, ht = products(a_blocks, a_cols, q_blocks, part_of, part_dest, part_pos, g_level, n_inner)
-    return merge(dense, h, ht, n_gx, n_inner, a_blocks.shape[2])
+    return hand_over(*merge(dense, h, ht, n_gx, n_inner, a_blocks.shape[2]))
 
 
 def solution(mesh):

time: 116 us -> 135 us (1.16)
  Pallas kernels: 111 us -> 134 us
  local copies, waits for them, and re-layouts: 3.83 us -> 0 us
    pallas_call x0 -> x1, Pallas kernels: none -> 36.9 us  [hand_over(): pl.pallas_call(hand_over_kernel, out_shape=(jax.ShapeDtypeStruct(first.sh...]
    pallas_call x1, Pallas kernels: 44.1 us -> 30.5 us  [products(): pl.pallas_call(products_kernel, grid=(fine // ROWS,), out_shape=(jax.Shap...]
    unnamed x2 -> x0, local copies, waits for them, and re-layouts: 3.83 us -> none
where the time goes in v6:
time: 135 us
  Pallas kernels  134 us (99%)
    pallas_call x1, Pallas kernels, merge(): pl.pallas_call(functools.partial(merge_kernel, n_gx, pieces, depth), out_...  66.8 us
    pallas_call x1, Pallas kernels, hand_over(): pl.pallas_call(hand_over_kernel, out_shape=(jax.ShapeDtypeStruct(first.sh...  36.9 us
    pallas_call x1, Pallas kernels, products(): pl.pallas_call(products_kernel, grid=(fine // ROWS,), out_shape=(jax.Shap...  30.5 us

profile of v6, /device:TPU:16, one launch (start us, length us, event | category | flops | bytes accessed | tf_op | source)
XLA Modules:
  0.0 134.8 jit_solution(2061146851356687916)
XLA Ops:
  0.6 30.5 %shard_map.86 = (f32[9216,128]{1,0:T(8,128)}, f32[128,128]{1,0:T(8,128)}, f32[96,96]{1,0:T(8,128)}) custom-call(bf16[64,8,9216]{2,1,0:T(8,128)(2,1)} %a_ref.1, bf16[64,9216]{1,0:T(8,128)(2,1)} %q_ref.1, f32[3,9216]{1,0:T(4,128)} %g_ref.1, s32[8,64]{1,0:T(8,128)} %bitcast.5, s32[8,64]{1,0:T(8,128)} %bitcast.6, s32[1,64]{1,0:T(1,128)} %bitcast.7, s32[64]{0:T(128)} %pos_ref.1), custom_call_target="tpu_custom_call" | custom-call | flops 1811939328 | bytes 9437184 | tf_op jit(solution)/shard_map/pallas_call | solution.py:147
  31.1 66.8 %shard_map.87 = (f32[2,8,9216]{2,1,0:T(8,128)}, f32[2,8,9216]{2,1,0:T(8,128)}) custom-call(f32[8,1152,128]{2,1,0:T(8,128)} %bitcast.4, f32[128,128]{1,0:T(8,128)} %get-tuple-element.8.h_ref, f32[96,96]{1,0:T(8,128)} %get-tuple-element.9.ht_ref), custom_call_target="tpu_custom_call" | custom-call | flops 56623104 | bytes 4718592 | tf_op jit(solution)/shard_map/pallas_call | solution.py:458
  97.9 36.9 %shard_map.88 = (f32[2,8,9216]{2,1,0:T(8,128)}, f32[2,8,9216]{2,1,0:T(8,128)}) custom-call(f32[2,8,9216]{2,1,0:T(8,128)} %get-tuple-element.10.first_in, f32[2,8,9216]{2,1,0:T(8,128)} %get-tuple-element.11.last_in), custom_call_target="tpu_custom_call" | custom-call | tf_op jit(solution)/shard_map/pallas_call | solution.py:508

commit v7 on v6

--- a/solution.py
+++ b/solution.py
@@ -13,7 +13,7 @@
 RC = 2
 SC = 8
 ROWS = 8
-UNROLL = 4
+UNROLL = 8
 F32 = jnp.float32
 BF16 = jnp.bfloat16
 
@@ -396,10 +396,10 @@
     for stage, at_edge, between in (
         (group_sums, 2, 0),
         (spread, 4, 0),
-        (descend, 6, 1),
-        (collect, 7, 3),
-        (fan_out, 9, busy),
-        (project, 10, busy),
+        (descend, 9, busy),
+        (collect, steps, busy),
+        (fan_out, steps, busy),
+        (project, steps, steps),
         (write_last, steps, steps),
     ):
         stage()
@@ -492,25 +492,19 @@
     )(dense.reshape(n_inner, owned, L), h, ht)
 
 
-def hand_over_kernel(first_in, last_in, first_ref, last_ref, sems):
-    copies = []
-    for r in range(RC):
-        copies.append(pltpu.make_async_copy(first_in.at[r], first_ref.at[r], sems.at[0, r]))
-        copies.append(pltpu.make_async_copy(last_in.at[r], last_ref.at[r], sems.at[1, r]))
-    for copy in copies:
-        copy.start()
-    for copy in copies:
-        copy.wait()
+def hand_over_kernel(first_in, last_in, first_ref, last_ref):
+    first_ref[...] = first_in[...]
+    last_ref[...] = last_in[...]
 
 
 def hand_over(first, last):
-    anywhere = pl.BlockSpec(memory_space=pl.ANY)
+    block = pl.BlockSpec((1, SC, first.shape[2]), lambda r: (r, 0, 0))
     return pl.pallas_call(
         hand_over_kernel,
+        grid=(RC,),
         out_shape=(jax.ShapeDtypeStruct(first.shape, F32), jax.ShapeDtypeStruct(last.shape, F32)),
-        in_specs=[anywhere, anywhere],
-        out_specs=(anywhere, anywhere),
-        scratch_shapes=[pltpu.SemaphoreType.DMA((2, RC))],
+        in_specs=[block, block],
+        out_specs=(block, block),
         compiler_params=pltpu.CompilerParams(vmem_limit_bytes=56 * 2**20),
     )(first, last)
 

time: 135 us -> 103 us (0.76)
  the two profiles are of different devices: /device:TPU:16 before, /device:TPU:1 now
where the time goes in v7:
time: 103 us
  Pallas kernels  103 us (100%)
    pallas_call x1, Pallas kernels, merge(): pl.pallas_call(functools.partial(merge_kernel, n_gx, pieces, depth), out_...  73.5 us
    pallas_call x1, Pallas kernels, products(): pl.pallas_call(products_kernel, grid=(fine // ROWS,), out_shape=(jax.Shap...  26.9 us
    pallas_call x1, Pallas kernels, hand_over(): pl.pallas_call(hand_over_kernel, grid=(RC,), out_shape=(jax.ShapeDtypeStr...  2.09 us

profile of v7, /device:TPU:1, one launch (start us, length us, event | category | flops | bytes accessed | tf_op | source)
XLA Modules:
  0.0 103.2 jit_solution(13665354526986532579)
XLA Ops:
  0.6 26.9 %shard_map.86 = (f32[9216,128]{1,0:T(8,128)}, f32[128,128]{1,0:T(8,128)}, f32[96,96]{1,0:T(8,128)}) custom-call(bf16[64,8,9216]{2,1,0:T(8,128)(2,1)} %a_ref.1, bf16[64,9216]{1,0:T(8,128)(2,1)} %q_ref.1, f32[3,9216]{1,0:T(4,128)} %g_ref.1, s32[8,64]{1,0:T(8,128)} %bitcast.5, s32[8,64]{1,0:T(8,128)} %bitcast.6, s32[1,64]{1,0:T(1,128)} %bitcast.7, s32[64]{0:T(128)} %pos_ref.1), custom_call_target="tpu_custom_call" | custom-call | flops 1811939328 | bytes 9437184 | tf_op jit(solution)/shard_map/pallas_call | solution.py:147
  27.6 73.5 %shard_map.87 = (f32[2,8,9216]{2,1,0:T(8,128)}, f32[2,8,9216]{2,1,0:T(8,128)}) custom-call(f32[8,1152,128]{2,1,0:T(8,128)} %bitcast.4, f32[128,128]{1,0:T(8,128)} %get-tuple-element.8.h_ref, f32[96,96]{1,0:T(8,128)} %get-tuple-element.9.ht_ref), custom_call_target="tpu_custom_call" | custom-call | flops 56623104 | bytes 4718592 | tf_op jit(solution)/shard_map/pallas_call | solution.py:458
  101.1 2.1 %shard_map.88 = (f32[2,8,9216]{2,1,0:T(8,128)}, f32[2,8,9216]{2,1,0:T(8,128)}) custom-call(f32[2,8,9216]{2,1,0:T(8,128)} %get-tuple-element.10.first_in, f32[2,8,9216]{2,1,0:T(8,128)} %get-tuple-element.11.last_in), custom_call_target="tpu_custom_call" | custom-call | tf_op jit(solution)/shard_map/pallas_call | solution.py:502
